TPU v7x, 256 devices: a whole 4x4x8 slice. The times are simulated.
256 devices in a mesh: dp: 16 (over z, core), sp: 16 (over x, y).
Axes of the slice: x: 4, y: 4, z: 8, core: 2. Of those that a mesh axis runs over, the one named last changes fastest.
Arguments:
- layer_input: bfloat16 [32768, 4096], P(('dp', 'sp')), may hold values from -24 to 24
- queries: bfloat16 [32768, 4096], P(('dp', 'sp')), may hold values from -36 to 36
- keys: bfloat16 [32768, 256], P(('dp', 'sp')), may hold values from -4 to 4
- values: bfloat16 [32768, 256], P(('dp', 'sp')), may hold values from -6 to 6
- out_grad: bfloat16 [32768, 4096], P(('dp', 'sp')), may hold values from -3 to 3
- key_value_weight: bfloat16 [4096, 512], P(('dp', 'sp')), may hold values from -0.09375 to 0.09375
Outputs:
- query_grad: bfloat16 [32768, 4096], P(('dp', 'sp'))
- input_grad: bfloat16 [32768, 4096], P(('dp', 'sp'))
- weight_grad: float32 [4096, 512], P(('dp', 'sp'))
All inputs are finite; a program needn't handle non-finite values.
Results may differ from a plain program's by a relative error of at most 0.015.
Values may be sent and summed in bfloat16 or wider, within the bound.
A program may use at most 128 MiB of HBM per device.

v0:
```python
import jax
import jax.numpy as jnp
from jax import lax
from jax.sharding import PartitionSpec as P

KEY_VALUE_HEADS = 2
HEAD_SIZE = 128


def body(layer_input, queries, keys, values, out_grad, key_value_weight):
    sequence_split_count = lax.axis_size("sp")
    dp_size = lax.axis_size("dp")
    token_rows = queries.shape[0]
    replica_list = sequence_split_count // KEY_VALUE_HEADS
    score_scale = HEAD_SIZE ** (-0.5)

    def spread(key_value_table):
        broadened_rows = jnp.broadcast_to(
            key_value_table.reshape(token_rows, KEY_VALUE_HEADS, 1, HEAD_SIZE),
            (token_rows, KEY_VALUE_HEADS, replica_list, HEAD_SIZE),
        )
        return broadened_rows.reshape(token_rows, sequence_split_count * HEAD_SIZE)

    q_heads, g_heads = (
        lax.all_to_all(queries, "sp", split_axis=1, concat_axis=0, tiled=True),
        lax.all_to_all(out_grad, "sp", split_axis=1, concat_axis=0, tiled=True),
    )
    k_heads, v_heads = (
        lax.all_to_all(spread(keys), "sp", split_axis=1, concat_axis=0, tiled=True),
        lax.all_to_all(spread(values), "sp", split_axis=1, concat_axis=0, tiled=True),
    )
    length = q_heads.shape[0]
    local_heads = q_heads.shape[1] // HEAD_SIZE
    q_three = q_heads.reshape(length, local_heads, HEAD_SIZE)
    g_three = g_heads.reshape(length, local_heads, HEAD_SIZE)
    fitting = [option_rows for option_rows in (512, 384, 256, 128) if length % option_rows == 0]
    block_rows = fitting[0]
    key_sum = jnp.zeros((length, HEAD_SIZE), jnp.float32)
    value_sum = jnp.zeros((length, HEAD_SIZE), jnp.float32)
    query_blocks = []
    for block_id in range(length // block_rows):
        first_row = block_id * block_rows
        last_row = first_row + block_rows
        q_block = q_three[first_row:last_row]
        g_block = g_three[first_row:last_row]
        key_rows = k_heads[:last_row]
        value_rows = v_heads[:last_row]
        scores = (
            jnp.einsum("qhd,kd->hqk", q_block, key_rows, preferred_element_type=jnp.float32)
            * score_scale
        )
        visible = jnp.arange(last_row)[None, :] <= (first_row + jnp.arange(block_rows))[:, None]
        scores = jnp.where(visible[None], scores, -jnp.inf)
        row_max = jnp.max(scores, axis=-1, keepdims=True)
        log_total = row_max + jnp.log(jnp.sum(jnp.exp(scores - row_max), axis=-1, keepdims=True))
        probs = jnp.exp(scores - log_total)
        dprobs = jnp.einsum("qhd,kd->hqk", g_block, value_rows, preferred_element_type=jnp.float32)
        row_dot = jnp.sum(probs * dprobs, axis=-1, keepdims=True)
        prob_low = probs.astype(jnp.bfloat16)
        dscore_low = (probs * (dprobs - row_dot)).astype(jnp.bfloat16)
        dq_block = (
            jnp.einsum("hqk,kd->qhd", dscore_low, key_rows, preferred_element_type=jnp.float32)
            * score_scale
        )
        query_blocks.append(
            dq_block.astype(jnp.bfloat16).reshape(block_rows, local_heads * HEAD_SIZE)
        )
        key_sum = key_sum.at[:last_row].add(
            jnp.einsum("hqk,qhd->kd", dscore_low, q_block, preferred_element_type=jnp.float32)
            * score_scale
        )
        value_sum = value_sum.at[:last_row].add(
            jnp.einsum("hqk,qhd->kd", prob_low, g_block, preferred_element_type=jnp.float32)
        )
    dq_heads = jnp.concatenate(query_blocks, axis=0)
    query_grad = lax.all_to_all(dq_heads, "sp", split_axis=0, concat_axis=1, tiled=True)
    key_low = key_sum.astype(jnp.bfloat16)
    value_low = value_sum.astype(jnp.bfloat16)
    paired = jnp.concatenate([key_low, value_low], axis=1)
    result_value = lax.all_to_all(paired, "sp", split_axis=0, concat_axis=1, tiled=True)
    gradient_total = (
        result_value.astype(jnp.float32)
        .reshape(token_rows, KEY_VALUE_HEADS, replica_list, 2, HEAD_SIZE)
        .sum(axis=2)
    )
    key_value_gradient = (
        gradient_total.transpose(0, 2, 1, 3)
        .reshape(token_rows, 2 * KEY_VALUE_HEADS * HEAD_SIZE)
        .astype(jnp.bfloat16)
    )
    input_grad = lax.dot_general(
        key_value_gradient,
        lax.all_gather(key_value_weight, ("dp", "sp"), axis=0, tiled=True),
        (((1,), (1,)), ((), ())),
        preferred_element_type=jnp.float32,
    ).astype(jnp.bfloat16)
    weight_sum = lax.psum_scatter(
        lax.dot_general(
            layer_input,
            key_value_gradient,
            (((0,), (0,)), ((), ())),
            preferred_element_type=jnp.float32,
        ),
        ("dp", "sp"),
        scatter_dimension=0,
        tiled=True,
    )
    weight_grad = weight_sum * (1.0 / dp_size)
    return (query_grad, input_grad, weight_grad)


def solution(mesh):
    placed = (
        P(("dp", "sp"), None),
        P(("dp", "sp"), None),
        P(("dp", "sp"), None),
        P(("dp", "sp"), None),
        P(("dp", "sp"), None),
        P(("dp", "sp"), None),
    )
    return jax.shard_map(
        body,
        mesh=mesh,
        in_specs=placed,
        out_specs=(P(("dp", "sp"), None), P(("dp", "sp"), None), P(("dp", "sp"), None)),
        check_vma=False,
    )
```

profile of v0, /device:TPU:0, one launch (start us, length us, event | category | flops | bytes accessed | tf_op | source)
XLA Modules:
  0.0 1465.1 jit_solution(13950624853312214415)
XLA Ops:
  9.1 5.3 all-to-all-start.2
  15.2 10.6 all-to-all-done.2
  26.8 3.6 all-to-all-start
  31.5 9.2 all-to-all-done
  40.7 3.7 all-to-all-start.1
  45.1 2.3 copy.193
  48.2 1.5 iota_compare_fusion.1
  49.7 9.5 all-to-all-done.1
  59.2 4.3 all-to-all-start.3
  72.7 5.6 all-to-all-done.3
  78.3 2.1 fusion.75
  93.3 1.7 fusion.8
  95.0 2.2 exponential_reduce_fusion
  97.3 1.6 fusion.9
  98.9 2.7 fusion.11
  101.6 2.5 fusion.56
  104.1 3.8 fusion.4
  107.9 6.2 fusion.6
  114.2 3.2 fusion.29
  117.4 2.9 fusion
  120.3 4.0 fusion.2
  124.4 3.9 fusion.42
  128.3 1.4 fusion.60
  131.1 2.9 fusion.39
  134.2 22.2 %all_to_all.102 = bf16[16,128,256]{1,2,0:T(8,128)(2,1)S(1)} all-to-all(bf16[16,128,256]{1,2,0:T(8,128)(2,1)S(1)} %copy_bitcast_fusion), channel_id=1, replica_groups=mesh['dp'=16,'sp'=16] {'sp'}, dimensions={0} | all-to-all | bytes 2097152 | tf_op jit(solution)/shard_map/all_to_all | solution.py:80
  156.8 4.5 convolution_bitcast_fusion
  161.3 9.0 copy.179
  171.3 2.5 fusion.65
  173.8 2.5 fusion.63
  177.8 17.8 %all_to_all.103 = bf16[16,128,256]{2,1,0:T(8,128)(2,1)S(1)} all-to-all(bf16[16,128,256]{2,1,0:T(8,128)(2,1)S(1)} %bitcast.258), channel_id=1, replica_groups=mesh['dp'=16,'sp'=16] {'sp'}, dimensions={0} | all-to-all | bytes 2097152 | tf_op jit(solution)/shard_map/all_to_all | solution.py:76
  197.6 4.7 convolution_convert_fusion
  202.2 1254.4 %reduce-scatter.4.cloned.1.call-done = f32[16,512]{1,0:T(8,128)} async-done(((f32[4096,512]{1,0:T(8,128)}), f32[16,512]{1,0:T(8,128)}) %reduce-scatter.4.cloned.1.call-update) | async-done | bytes 32784
  (135 shorter events, 36.0 us)
Async XLA Ops:
  7.2 149.6 %copy-start = (bf16[128,4096]{1,0:T(8,128)(2,1)S(1)}, bf16[128,4096]{1,0:T(8,128)(2,1)}, u32[]{:S(2)}) copy-start(bf16[128,4096]{1,0:T(8,128)(2,1)} %param.26) | copy-start | bytes 3145732
  7.2 23.3 %copy-start.24 = (bf16[128,4096]{1,0:T(8,128)(2,1)S(1)}, bf16[128,4096]{1,0:T(8,128)(2,1)}, u32[]{:S(2)}) copy-start(bf16[128,4096]{1,0:T(8,128)(2,1)} %param.27) | copy-start | bytes 3145732
  9.1 16.8 %all-to-all-start.2 = ((bf16[128,16,128]{2,0,1:T(8,128)(2,1)}), bf16[128,16,128]{2,0,1:T(8,128)(2,1)S(1)}, u32[]{:S(2)}, u32[]{:S(2)}) async-start(bf16[128,16,128]{2,0,1:T(8,128)(2,1)} %bitcast.6), calls=%async_computation.2 | async-start | bytes 1048576 | tf_op jit(solution)/shard_map/all_to_all | solution.py:30
  25.9 41.3 %copy-start.6 = (bf16[128,16,128]{2,0,1:T(8,128)(2,1)}, bf16[128,16,128]{2,0,1:T(8,128)(2,1)S(1)}, u32[]{:S(2)}) copy-start(bf16[128,16,128]{2,0,1:T(8,128)(2,1)S(1)} %all-to-all-done.2) | copy-start | bytes 1572868
  26.8 13.8 all-to-all-start
  40.7 28.1 %copy-start.10 = (bf16[128,16,128]{2,0,1:T(8,128)(2,1)}, bf16[128,16,128]{2,0,1:T(8,128)(2,1)S(1)}, u32[]{:S(2)}) copy-start(bf16[128,16,128]{2,0,1:T(8,128)(2,1)S(1)} %all-to-all-done) | copy-start | bytes 1572868
  40.7 18.5 %all-to-all-start.1 = ((bf16[128,16,256]{2,0,1:T(8,128)(2,1)}), bf16[128,16,256]{2,0,1:T(8,128)(2,1)S(1)}, u32[]{:S(2)}, u32[]{:S(2)}) async-start(bf16[128,16,256]{2,0,1:T(8,128)(2,1)} %bitcast.256), calls=%async_computation.1 | async-start | bytes 2097152 | tf_op jit(solution)/shard_map/all_to_all | solution.py:25
  44.4 153.2 %all-gather.2.cloned.1.call-start = ((), (), s32[]{:S(2)}) async-start(), calls=%async_computation.7 | async-start | bytes 4210688 | tf_op jit(solution)/shard_map/all_gather | solution.py:93
  59.2 4.6 copy-start.8
  59.2 19.1 %all-to-all-start.3 = ((bf16[128,16,256]{2,0,1:T(8,128)(2,1)}), bf16[128,16,256]{2,0,1:T(8,128)(2,1)}, u32[]{:S(2)}, u32[]{:S(2)}) async-start(bf16[128,16,256]{2,0,1:T(8,128)(2,1)} %bitcast.248), calls=%async_computation.3 | async-start | bytes 2097152 | tf_op jit(solution)/shard_map/all_to_all | solution.py:26
  63.6 1393.0 %reduce-scatter.4.cloned.1.call-start = ((), (), s32[]{:S(2)}) async-start(), calls=%async_computation.8 | async-start | bytes 8421376
  65.0 4.5 copy-start.9
  69.9 14.8 %copy-start.14 = (bf16[512,2,128]{0,2,1:T(8,128)(2,1)}, bf16[512,2,128]{0,2,1:T(8,128)(2,1)S(1)}, u32[]{:S(2)}) copy-start(bf16[512,2,128]{0,2,1:T(8,128)(2,1)S(1)} %copy.139) | copy-start | bytes 786436
  70.8 13.8 copy-start.26
  86.5 2.3 copy-start.4
  86.6 2.3 copy-start.25
  86.6 2.3 copy-start.31
  88.9 1.9 copy-start.21
  89.8 9.0 copy-start.1
  95.0 2.2 copy-start.20
  95.0 2.2 copy-start.22
  98.9 5.2 copy-start.16
  114.2 3.2 copy-start.7
  114.2 3.2 copy-start.17
  120.3 4.0 copy-start.19
  124.3 3.9 copy-start.2
  124.3 3.9 copy-start.5
  124.3 3.9 copy-start.13
  124.3 3.9 copy-start.23
  170.3 3.5 copy-start.30
  170.3 6.0 copy-start.3
  170.3 6.0 copy-start.12
  (7 other events, 9.5 us)
Sparse Core Ops, SparseCore 0:
  48.8 121.3 all-gather.1
  172.7 1283.9 reduce-scatter.3
where the time goes:
time: 1470 us
  waiting for transfers between devices  1290 us (88%)
  matrix products  44.7 us (3%)
  blocking collectives  40 us (3%)
  local copies, waits for them, and re-layouts  35.6 us (2%)
  other arithmetic  22.8 us (2%)
  starting transfers between devices  17.1 us (1%)
  between operations  14.8 us (1%)
    unnamed x3, waiting for transfers between devices  1260 us
  transfers between devices with their start and end apart: 6, of which 5 were waited for; matrix products, arithmetic and copies ran while one was open for 7% of the time, Pallas kernels for 0%

commit v1 on v0

v1 whole, which is shorter than its diff:
```python
import functools
import math

import jax
import jax.numpy as jnp
from jax import lax
from jax.experimental import pallas as pl
from jax.experimental.pallas import tpu as pltpu
from jax.sharding import PartitionSpec as P

HEAD = 128
SCALE = HEAD ** -0.5
SCALE2 = SCALE * math.log2(math.e)
HEADS_AT_ONCE = 4
KEY_ROWS = 1024
f32 = jnp.float32
bf16 = jnp.bfloat16


def dot(a, b, ca, cb):
    return lax.dot_general(a, b, (((ca,), (cb,)), ((), ())), preferred_element_type=f32)


def attend(s, gi, group, q_ref, g_ref, kv_ref, dq_ref, s_scr, dp_scr, dk_scr, dv_scr, kt_scr, dqt_scr):
    tokens = q_ref.shape[0]
    rows = HEADS_AT_ONCE * tokens
    chunks = (s * tokens) // KEY_ROWS + 1
    kcols = pl.ds(gi * HEAD, HEAD)
    vcols = pl.ds((2 + gi) * HEAD, HEAD)

    def keys_of(c):
        return pl.ds(pl.multiple_of(c * KEY_ROWS, KEY_ROWS), KEY_ROWS)

    def prepare(c, _):
        r = keys_of(c)
        kt_scr[:, r] = kv_ref[r, kcols].T
        return 0

    lax.fori_loop(0, chunks, prepare, 0)
    dk_scr[...] = jnp.zeros_like(dk_scr)
    dv_scr[...] = jnp.zeros_like(dv_scr)

    def heads(hb, _):
        first = gi * group + hb * HEADS_AT_ONCE
        cols = [pl.ds(pl.multiple_of((first + i) * HEAD, HEAD), HEAD) for i in range(HEADS_AT_ONCE)]
        q = jnp.concatenate([q_ref[:, h] for h in cols], axis=0)
        g = jnp.concatenate([g_ref[:, h] for h in cols], axis=0)
        qf = q.astype(f32) * SCALE2
        high = qf.astype(bf16)
        low = (qf - high.astype(f32)).astype(bf16)
        q2 = jnp.concatenate([high, low], axis=1)

        def score(c):
            r = keys_of(c)
            k = kv_ref[r, kcols]
            return r, dot(jnp.concatenate([k, k], axis=1), q2, 1, 1)

        def top(x):
            return x.reshape(KEY_ROWS // 8, 8, rows).max(0)

        def add(x):
            return x.reshape(KEY_ROWS // 8, 8, rows).sum(0)

        def first_pass(c, m):
            r, sc = score(c)
            s_scr[r, :] = sc
            return jnp.maximum(m, top(sc))

        m = lax.fori_loop(0, chunks - 1, first_pass, jnp.full((8, rows), -jnp.inf, f32))
        r, sc = score(chunks - 1)
        key = (chunks - 1) * KEY_ROWS + lax.broadcasted_iota(jnp.int32, (KEY_ROWS, rows), 0)
        token = s * tokens + lax.broadcasted_iota(jnp.int32, (KEY_ROWS, rows), 1) % tokens
        sc = jnp.where(key <= token, sc, -jnp.inf)
        s_scr[r, :] = sc
        m = jnp.maximum(m, top(sc)).max(0, keepdims=True)

        def second_pass(c, carry):
            total, rd = carry
            r = keys_of(c)
            e = jnp.exp2(s_scr[r, :] - m)
            s_scr[r, :] = e
            dp = dot(kv_ref[r, vcols], g, 1, 1)
            dp_scr[r, :] = dp
            return total + add(e), rd + add(e * dp)

        zero = jnp.zeros((8, rows), f32)
        total, rd = lax.fori_loop(0, chunks, second_pass, (zero, zero))
        inv = 1.0 / total.sum(0, keepdims=True)
        rd = rd.sum(0, keepdims=True) * inv
        dqt_scr[...] = jnp.zeros_like(dqt_scr)

        def third_pass(c, _):
            r = keys_of(c)
            p = s_scr[r, :] * inv
            ds = (p * (dp_scr[r, :] - rd)).astype(bf16)
            dv_scr[r, :] += dot(p.astype(bf16), g, 1, 0)
            dk_scr[r, :] += dot(ds, q, 1, 0)
            dqt_scr[...] += dot(kt_scr[:, r], ds, 1, 0)
            return 0

        lax.fori_loop(0, chunks, third_pass, 0)
        dq = (dqt_scr[...] * SCALE).T.astype(bf16)
        for i in range(HEADS_AT_ONCE):
            dq_ref[:, cols[i]] = dq[i * tokens : (i + 1) * tokens]
        return 0

    lax.fori_loop(0, group // HEADS_AT_ONCE, heads, 0)


def attention_kernel(q_ref, g_ref, kv_ref, dq_ref, part_ref, s_scr, dp_scr, dk_scr, dv_scr, kt_scr, dqt_scr):
    s = lax.axis_index("sp")
    for gi in range(2):
        attend(s, gi, 16, q_ref, g_ref, kv_ref, dq_ref, s_scr, dp_scr, dk_scr, dv_scr, kt_scr, dqt_scr)
        part_ref[:, gi * HEAD : (gi + 1) * HEAD] = (dk_scr[...] * SCALE).astype(bf16)
        part_ref[:, (2 + gi) * HEAD : (3 + gi) * HEAD] = dv_scr[...].astype(bf16)


def body(layer_input, queries, keys, values, out_grad, key_value_weight):
    n_sp = lax.axis_size("sp")
    n_dp = lax.axis_size("dp")
    tokens, width = queries.shape
    length = tokens * n_sp
    rows = HEADS_AT_ONCE * tokens
    kv = lax.all_gather(jnp.concatenate([keys, values], axis=1), "sp", axis=0, tiled=True)
    vmem = pl.BlockSpec(memory_space=pltpu.VMEM)
    query_grad, part = pl.pallas_call(
        attention_kernel,
        out_shape=[
            jax.ShapeDtypeStruct((tokens, width), bf16),
            jax.ShapeDtypeStruct((length, 4 * HEAD), bf16),
        ],
        in_specs=[vmem] * 3,
        out_specs=[vmem] * 2,
        scratch_shapes=[
            pltpu.VMEM((length, rows), f32),
            pltpu.VMEM((length, rows), f32),
            pltpu.VMEM((length, HEAD), f32),
            pltpu.VMEM((length, HEAD), f32),
            pltpu.VMEM((HEAD, length), bf16),
            pltpu.VMEM((HEAD, rows), f32),
        ],
        compiler_params=pltpu.CompilerParams(vmem_limit_bytes=48 * 2**20),
        cost_estimate=pl.CostEstimate(flops=10 * 2**30, bytes_accessed=8 * 2**20, transcendentals=8 * 2**20),
        name="attention",
    )(queries, out_grad, kv)
    moved = lax.all_to_all(part.reshape(n_sp, tokens, 4 * HEAD), "sp", split_axis=0, concat_axis=0)
    kv_grad = moved.astype(f32).sum(axis=0).astype(bf16)
    spread = layer_input.T.reshape(n_dp, n_sp, width // (n_dp * n_sp), tokens)
    columns = lax.all_to_all(spread, "sp", split_axis=1, concat_axis=1)
    columns = columns.transpose(0, 2, 1, 3).reshape(width // n_sp, length)
    weight = lax.all_gather(key_value_weight, ("dp", "sp"), axis=0, tiled=True)
    kv_grad_all = lax.all_gather(kv_grad, "sp", axis=0, tiled=True)
    input_grad = dot(kv_grad, weight, 1, 1).astype(bf16)
    partial = dot(columns, kv_grad_all, 1, 0).reshape(n_dp, width // (n_dp * n_sp), 4 * HEAD)
    partial = lax.all_to_all(partial, "dp", split_axis=0, concat_axis=0)
    weight_grad = partial.sum(axis=0) * (1.0 / n_dp)
    return query_grad, input_grad, weight_grad


def solution(mesh):
    placed = P(("dp", "sp"), None)
    return jax.shard_map(
        body,
        mesh=mesh,
        in_specs=(placed,) * 6,
        out_specs=(placed,) * 3,
        check_vma=False,
    )
```

time: 1470 us -> 315 us (0.21)
  the two profiles are of different devices: /device:TPU:0 before, /device:TPU:1 now
where the time goes in v1:
time: 315 us
  waiting for transfers between devices  195 us (62%)
  blocking collectives  62.1 us (20%)
  Pallas kernels  19.9 us (6%)
  between operations  13.8 us (4%)
  starting transfers between devices  8.64 us (3%)
  matrix products  7.8 us (2%)
  local copies, waits for them, and re-layouts  4.06 us (1%)
  other arithmetic  3.15 us (1%)
    all_gather x1, waiting for transfers between devices, body(): weight = lax.all_gather(key_value_weight, ('dp', 'sp'), axis=0, tiled=True)  108 us
    all_gather x1, waiting for transfers between devices, body(): lax.all_gather(jnp.concatenate([keys, values], axis=1), 'sp', axis=0, til...  55.1 us
    all_to_all x1, blocking collectives, body(): lax.all_to_all(part.reshape(n_sp, tokens, 4 * HEAD), 'sp', split_axis=0,...  45.1 us
    all_gather x1, waiting for transfers between devices, body(): kv_grad_all = lax.all_gather(kv_grad, 'sp', axis=0, tiled=True)  31.5 us
    pallas_call x1, Pallas kernels, body(): pl.pallas_call(attention_kernel, out_shape=[jax.ShapeDtypeStruct((tokens,...  19.9 us
    all_to_all x1, blocking collectives, body(): columns = lax.all_to_all(spread, 'sp', split_axis=1, concat_axis=1)  17 us
    all_to_all x1, starting transfers between devices, body(): partial = lax.all_to_all(partial, 'dp', split_axis=0, concat_axis=0)  8.52 us
    dot_general x2, matrix products, dot(): lax.dot_general(a, b, (((ca,), (cb,)), ((), ())), preferred_element_type=...  7.8 us
  transfers between devices with their start and end apart: 4, of which 3 were waited for; matrix products, arithmetic and copies ran while one was open for 3% of the time, Pallas kernels for 0%

profile of v1, /device:TPU:1, one launch (start us, length us, event | category | flops | bytes accessed | tf_op | source)
XLA Modules:
  0.0 314.7 jit_solution(12656633000585020269)
XLA Ops:
  7.2 0.0 all-gather.4.cloned.1.call-start
  7.2 1.5 pad_maximum_fusion
  8.7 0.0 all-gather.4.cloned.1.call-update
  8.8 0.0 all-gather.8.cloned.1.call-start
  8.8 55.1 %all-gather.4.cloned.1.call-done.kv_ref = bf16[2048,512]{1,0:T(8,128)(2,1)} async-done(((bf16[128,512]{1,0:T(8,128)(2,1)}), bf16[2048,512]{1,0:T(8,128)(2,1)}) %all-gather.4.cloned.1.call-update) | async-done | bytes 2097168 | tf_op jit(solution)/shard_map/all_gather | solution.py:124
  63.9 0.0 copy-start
  64.0 1.2 copy-done
  65.2 0.0 copy-start.1
  65.2 1.2 copy-done.1
  66.4 19.9 %attention.1 = (bf16[128,4096]{1,0:T(8,128)(2,1)}, bf16[2048,512]{1,0:T(8,128)(2,1)S(1)}) custom-call(bf16[128,4096]{1,0:T(8,128)(2,1)S(1)} %copy-done, bf16[128,4096]{1,0:T(8,128)(2,1)S(1)} %copy-done.1, bf16[2048,512]{1,0:T(8,128)(2,1)} %all-gather.4.cloned.1.call-done.kv_ref), custom_call_target="tpu_custom_call" | custom-call | flops 10737418240 | bytes 8388608 | tf_op jit(solution)/shard_map/attention/pallas_call | solution.py:126
  86.2 45.1 %all_to_all.15 = bf16[16,128,512]{2,1,0:T(8,128)(2,1)S(1)} all-to-all(bf16[16,128,512]{2,1,0:T(8,128)(2,1)S(1)} %bitcast.16), channel_id=1, replica_groups=mesh['dp'=16,'sp'=16] {'sp'}, dimensions={0} | all-to-all | bytes 4194304 | tf_op jit(solution)/shard_map/all_to_all | solution.py:146
  131.4 0.0 copy-start.3
  131.4 1.0 reduce_sum.21
  132.3 0.0 all-gather.8.cloned.1.call-update
  132.3 0.0 all-gather.6.cloned.1.call-start
  132.4 0.7 all-gather.6.cloned.1.call-update
  133.1 0.0 copy-done.3
  133.1 0.7 copy.11
  133.8 0.3 copy.12
  134.0 17.0 %all_to_all.16 = bf16[16,16,16,128]{3,2,0,1:T(8,128)(2,1)S(1)} all-to-all(bf16[16,16,16,128]{3,2,0,1:T(8,128)(2,1)S(1)} %copy.12), channel_id=1, replica_groups=mesh['dp'=16,'sp'=16] {'sp'}, dimensions={1} | all-to-all | bytes 2097152 | tf_op jit(solution)/shard_map/all_to_all | solution.py:149
  151.0 0.7 copy.13
  151.7 31.5 %all-gather.8.cloned.1.call-done = bf16[2048,512]{1,0:T(8,128)(2,1)} async-done(((bf16[128,512]{1,0:T(8,128)(2,1)}), bf16[2048,512]{1,0:T(8,128)(2,1)}) %all-gather.8.cloned.1.call-update) | async-done | bytes 2097168 | tf_op jit(solution)/shard_map/all_gather | solution.py:152
  183.2 0.0 copy-start.2
  183.2 3.2 %fusion = f32[512,256]{0,1:T(8,128)} fusion(bf16[2048,512]{1,0:T(8,128)(2,1)} %all-gather.8.cloned.1.call-done, bf16[32,8,16,128]{3,2,1,0:T(8,128)(2,1)S(1)} %bitcast.19), kind=kOutput, calls=%fused_computation.1 | convolution fusion | flops 536870912 | bytes 3670016 | tf_op jit(solution)/shard_map/dot_general | solution.py:21
  186.4 8.5 %all-to-all-start.2 = ((f32[16,16,512]{2,1,0:T(8,128)}), f32[16,16,512]{2,1,0:T(8,128)S(1)}, u32[]{:S(2)}, u32[]{:S(2)}) async-start(f32[16,16,512]{2,1,0:T(8,128)} %bitcast.5), calls=%async_computation.2 | async-start | bytes 1048576 | tf_op jit(solution)/shard_map/all_to_all | solution.py:155
  194.9 108.0 %all-gather.6.cloned.1.call-done = bf16[4096,512]{1,0:T(8,128)(2,1)} async-done(((bf16[16,512]{1,0:T(8,128)(2,1)}), bf16[4096,512]{1,0:T(8,128)(2,1)}) %all-gather.6.cloned.1.call-update) | async-done | bytes 4194320 | tf_op jit(solution)/shard_map/all_gather | solution.py:151
  302.9 0.0 copy-done.2
  302.9 4.6 %convolution_convert_fusion = bf16[128,4096]{1,0:T(8,128)(2,1)} fusion(bf16[128,512]{1,0:T(8,128)(2,1)S(1)} %copy-done.2, bf16[4096,512]{1,0:T(8,128)(2,1)} %all-gather.6.cloned.1.call-done), kind=kOutput, calls=%fused_computation | convolution fusion | flops 537395200 | bytes 5373952 | tf_op jit(solution)/shard_map/dot_general | solution.py:21
  307.5 0.0 all-to-all-done.2
  307.6 0.6 broadcast_multiply_fusion
  (1 shorter events, 0.0 us)
Async XLA Ops:
  7.2 56.8 %all-gather.4.cloned.1.call-start = ((), (), s32[]{:S(2)}) async-start(), calls=%async_computation.3 | async-start | bytes 2228224 | tf_op jit(solution)/shard_map/all_gather | solution.py:124
  8.8 174.5 %all-gather.8.cloned.1.call-start = ((), (), s32[]{:S(2)}) async-start(), calls=%async_computation.5 | async-start | bytes 2228224 | tf_op jit(solution)/shard_map/all_gather | solution.py:152
  63.9 1.2 copy-start
  65.2 1.2 copy-start.1
  131.4 1.7 copy-start.3
  132.3 170.6 %all-gather.6.cloned.1.call-start = ((), (), s32[]{:S(2)}) async-start(), calls=%async_computation.4 | async-start | bytes 4210688 | tf_op jit(solution)/shard_map/all_gather | solution.py:151
  183.2 119.7 %copy-start.2 = (bf16[128,512]{1,0:T(8,128)(2,1)S(1)}, bf16[128,512]{1,0:T(8,128)(2,1)}, u32[]{:S(2)}) copy-start(bf16[128,512]{1,0:T(8,128)(2,1)} %reduce_sum.21) | copy-start | bytes 393220
  186.4 121.1 %all-to-all-start.2 = ((f32[16,16,512]{2,1,0:T(8,128)}), f32[16,16,512]{2,1,0:T(8,128)S(1)}, u32[]{:S(2)}, u32[]{:S(2)}) async-start(f32[16,16,512]{2,1,0:T(8,128)} %bitcast.5), calls=%async_computation.2 | async-start | bytes 1048576 | tf_op jit(solution)/shard_map/all_to_all | solution.py:155
Sparse Core Ops, SparseCore 0:
  11.0 52.8 all-gather.3
  132.5 50.7 all-gather.7
  186.8 116.0 all-gather.5

commit v2 on v1

v2 whole, which is shorter than its diff:
```python
import functools
import math

import jax
import jax.numpy as jnp
from jax import lax
from jax.experimental import pallas as pl
from jax.experimental.pallas import tpu as pltpu
from jax.sharding import PartitionSpec as P

HEAD = 128
SCALE = HEAD ** -0.5
SCALE2 = SCALE * math.log2(math.e)
HEADS_AT_ONCE = 4
KEY_ROWS = 1024
f32 = jnp.float32
bf16 = jnp.bfloat16


def dot(a, b, ca, cb):
    return lax.dot_general(a, b, (((ca,), (cb,)), ((), ())), preferred_element_type=f32)


def attend_heads(s, first, key_rows, q_ref, g_ref, kv_ref, dq_ref, s_scr, dp_scr, dk_scr, dv_scr, kt_scr, dqt_scr):
    tokens = q_ref.shape[0]
    rows = HEADS_AT_ONCE * tokens
    chunks = (s * tokens) // key_rows + 1

    def keys_of(c):
        return pl.ds(pl.multiple_of(c * key_rows, key_rows), key_rows)

    cols = [pl.ds(pl.multiple_of((first + i) * HEAD, HEAD), HEAD) for i in range(HEADS_AT_ONCE)]
    q = jnp.concatenate([q_ref[:, h] for h in cols], axis=0)
    g = jnp.concatenate([g_ref[:, h] for h in cols], axis=0)
    qf = q.astype(f32) * SCALE2
    high = qf.astype(bf16)
    low = (qf - high.astype(f32)).astype(bf16)
    q2 = jnp.concatenate([high, low], axis=1)

    def score(c):
        r = keys_of(c)
        k = kv_ref[r, :HEAD]
        return r, dot(jnp.concatenate([k, k], axis=1), q2, 1, 1)

    def top(x):
        return x.reshape(key_rows // 8, 8, rows).max(0)

    def add(x):
        return x.reshape(key_rows // 8, 8, rows).sum(0)

    def first_pass(c, m):
        r, sc = score(c)
        s_scr[r, :] = sc
        return jnp.maximum(m, top(sc))

    m = lax.fori_loop(0, chunks - 1, first_pass, jnp.full((8, rows), -jnp.inf, f32))
    r, sc = score(chunks - 1)
    key = (chunks - 1) * key_rows + lax.broadcasted_iota(jnp.int32, (key_rows, rows), 0)
    token = s * tokens + lax.broadcasted_iota(jnp.int32, (key_rows, rows), 1) % tokens
    sc = jnp.where(key <= token, sc, -jnp.inf)
    s_scr[r, :] = sc
    m = jnp.maximum(m, top(sc)).max(0, keepdims=True)

    def second_pass(c, carry):
        total, rd = carry
        r = keys_of(c)
        e = jnp.exp2(s_scr[r, :] - m)
        s_scr[r, :] = e
        dp = dot(kv_ref[r, HEAD:], g, 1, 1)
        dp_scr[r, :] = dp
        return total + add(e), rd + add(e * dp)

    zero = jnp.zeros((8, rows), f32)
    total, rd = lax.fori_loop(0, chunks, second_pass, (zero, zero))
    inv = 1.0 / total.sum(0, keepdims=True)
    rd = rd.sum(0, keepdims=True) * inv
    dqt_scr[...] = jnp.zeros_like(dqt_scr)

    def third_pass(c, _):
        r = keys_of(c)
        p = s_scr[r, :] * inv
        ds = (p * (dp_scr[r, :] - rd)).astype(bf16)
        dv_scr[r, :] += dot(p.astype(bf16), g, 1, 0)
        dk_scr[r, :] += dot(ds, q, 1, 0)
        dqt_scr[...] += dot(kt_scr[:, r], ds, 1, 0)
        return 0

    lax.fori_loop(0, chunks, third_pass, 0)
    dq = (dqt_scr[...] * SCALE).T.astype(bf16)
    for i in range(HEADS_AT_ONCE):
        dq_ref[:, cols[i]] = dq[i * tokens : (i + 1) * tokens]


def kernel(
    n_dp, n_sp,
    x_ref, q_ref, k_ref, v_ref, g_ref, w_ref,
    dq_ref, ig_ref, wg_ref,
    s_scr, dp_scr, dk_scr, dv_scr, kt_scr, dqt_scr,
    kv_all, xt, x_all, w_all, part, part_in, grad_all, sum_scr, row_out, row_in,
    kv_send, kv_recv, x_send, x_recv, w_send, w_recv, right_send, left_send, ring_recv, pair_send, pair_recv,
    part_send, part_recv, grad_send, grad_recv, row_send, row_recv,
):
    d = lax.axis_index("dp")
    s = lax.axis_index("sp")
    n_z = n_dp // 2
    z, core = d // 2, d % 2
    tokens = q_ref.shape[0]
    length = tokens * n_sp
    key_rows = min(KEY_ROWS, length)
    group = q_ref.shape[1] // HEAD // 2
    per_group = group // HEADS_AT_ONCE
    w_rows = w_ref.shape[0]
    block = n_sp * w_rows

    barrier = pltpu.get_barrier_semaphore()

    def greet(n, me, axis):
        def one(i, _):
            pl.semaphore_signal(
                barrier, inc=1, device_id={axis: lax.rem(me + i, n)}, device_id_type=pl.DeviceIdType.MESH
            )
            return 0

        lax.fori_loop(1, n, one, 0)

    greet(n_sp, s, "sp")
    greet(n_dp, d, "dp")

    def copy(src, dst, send, recv, axis, to):
        return pltpu.make_async_remote_copy(
            src_ref=src, dst_ref=dst, send_sem=send, recv_sem=recv,
            device_id={axis: to}, device_id_type=pl.DeviceIdType.MESH,
        )

    def each_sp(f):
        def one(i, _):
            f(lax.rem(s + i, n_sp))
            return 0

        lax.fori_loop(1, n_sp, one, 0)

    def each_dp(f):
        def one(i, _):
            f(lax.rem(d + i, n_dp))
            return 0

        lax.fori_loop(1, n_dp, one, 0)

    def span(i, size):
        return pl.ds(pl.multiple_of(i * size, size), size)

    own = span(s, tokens)

    def kv_copy(gi, t, owner):
        r = span(owner, tokens)
        return copy(kv_all.at[gi, r], kv_all.at[gi, r], kv_send.at[gi, t], kv_recv.at[gi, owner], "sp", t)

    def w_copy(t, owner):
        r = pl.ds(pl.multiple_of(d * block + owner * w_rows, w_rows), w_rows)
        return copy(w_all.at[r], w_all.at[r], w_send.at[t], w_recv.at[owner], "sp", t)

    def ring_copy(zb, to, send):
        r = span(zb * 2 + core, block)
        return copy(w_all.at[r], w_all.at[r], send, ring_recv.at[zb], "dp", to * 2 + core)

    def pair_copy(zb, c):
        r = span(zb * 2 + c, block)
        return copy(w_all.at[r], w_all.at[r], pair_send.at[zb], pair_recv.at[zb], "dp", z * 2 + 1 - core)

    def x_copy(t, owner):
        return copy(xt.at[t], x_all.at[owner], x_send.at[t], x_recv.at[owner], "sp", t)

    def part_copy(gi, t, owner):
        return copy(part.at[gi, t], part_in.at[gi, owner], part_send.at[gi, t], part_recv.at[gi, owner], "sp", t)

    def grad_copy(gi, t, owner):
        return copy(
            grad_all.at[gi, owner], grad_all.at[gi, owner], grad_send.at[gi, t], grad_recv.at[gi, owner], "sp", t
        )

    def row_copy(gi, t, owner):
        return copy(
            row_out.at[gi, span(t, w_rows)], row_in.at[gi, owner], row_send.at[gi, t], row_recv.at[gi, owner], "dp", t
        )

    for gi in range(2):
        kv_all[gi, own, :HEAD] = k_ref[:, gi * HEAD : (gi + 1) * HEAD]
        kv_all[gi, own, HEAD:] = v_ref[:, gi * HEAD : (gi + 1) * HEAD]

        def clear(t, _):
            kv_all[gi, span(t, tokens)] = jnp.zeros((tokens, 2 * HEAD), bf16)
            return 0

        lax.fori_loop(s + 1, n_sp, clear, 0)
    w_all[pl.ds(pl.multiple_of(d * block + s * w_rows, w_rows), w_rows)] = w_ref[...]
    pl.semaphore_wait(barrier, n_sp + n_dp - 2)

    for gi in range(2):

        def send_kv(t, _):
            kv_copy(gi, t, s).start()
            return 0

        lax.fori_loop(s + 1, n_sp, send_kv, 0)
    each_sp(lambda t: w_copy(t, s).start())

    def transpose(j, _):
        columns = x_ref[:, span(j, block)].T
        xt[:, span(j, w_rows)] = columns.reshape(n_sp, w_rows, tokens)
        return 0

    lax.fori_loop(0, n_dp, transpose, 0)
    x_all[s] = xt[s]
    each_sp(lambda t: x_copy(t, s).start())

    right = lax.rem(z + 1, n_z)
    left = lax.rem(z + n_z - 1, n_z)
    n_right = n_z // 2
    n_left = n_z - 1 - n_right

    def ring_step(k):
        @pl.when(k == 0)
        def _():
            each_sp(lambda t: w_copy(s, t).wait_recv())
            ring_copy(z, right, right_send.at[0]).start()
            if n_left:
                ring_copy(z, left, left_send.at[0]).start()
            pair_copy(z, core).start()

        @pl.when((k >= 1) & (k <= n_right))
        def _():
            zb = lax.rem(z + n_z - k, n_z)
            ring_copy(zb, right, right_send.at[0]).wait_recv()

            @pl.when(k < n_right)
            def _():
                ring_copy(zb, right, right_send.at[k]).start()

            pair_copy(zb, core).start()

        @pl.when((k >= 1) & (k <= n_left))
        def _():
            zb = lax.rem(z + k, n_z)
            ring_copy(zb, left, left_send.at[0]).wait_recv()

            @pl.when(k < n_left)
            def _():
                ring_copy(zb, left, left_send.at[k]).start()

            pair_copy(zb, core).start()

    def reduce(gi):
        def one(t, _):
            part_copy(gi, s, t).wait_recv()
            sum_scr[:tokens] += part_in[gi, t].astype(f32)
            return 0

        sum_scr[:tokens] = part[gi, s].astype(f32)
        lax.fori_loop(s + 1, n_sp, one, 0)
        grad_all[gi, s] = sum_scr[:tokens].astype(bf16)
        each_sp(lambda t: grad_copy(gi, t, s).start())

    steps = 2 * per_group
    for gi in range(2):

        def wait_kv(t, _):
            kv_copy(gi, s, t).wait_recv()
            return 0

        lax.fori_loop(0, s, wait_kv, 0)

        def prepare(c, _):
            r = span(c, key_rows)
            kt_scr[:, r] = kv_all[gi, r, :HEAD].T
            dk_scr[r] = jnp.zeros((key_rows, HEAD), f32)
            dv_scr[r] = jnp.zeros((key_rows, HEAD), f32)
            return 0

        lax.fori_loop(0, length // key_rows, prepare, 0)

        def heads(hb, _):
            it = gi * per_group + hb

            @pl.when(it >= 1)
            def _():
                ring_step(it - 1)

            if gi == 1:

                @pl.when(it == steps * 3 // 4)
                def _():
                    reduce(0)

            attend_heads(
                s, gi * group + hb * HEADS_AT_ONCE, key_rows,
                q_ref, g_ref, kv_all.at[gi], dq_ref, s_scr, dp_scr, dk_scr, dv_scr, kt_scr, dqt_scr,
            )
            return 0

        lax.fori_loop(0, per_group, heads, 0)

        def give(t, _):
            r = span(t, tokens)
            part[gi, t, :, :HEAD] = (dk_scr[r] * SCALE).astype(bf16)
            part[gi, t, :, HEAD:] = dv_scr[r].astype(bf16)

            @pl.when(t < s)
            def _():
                part_copy(gi, t, s).start()

            return 0

        lax.fori_loop(0, s + 1, give, 0)

    for k in range(steps - 1, n_right + 1):
        ring_step(k)

    def weight_rows(gi):
        each_sp(lambda t: grad_copy(gi, s, t).wait_recv())
        sum_scr[...] = jnp.zeros_like(sum_scr)

        def one(i, _):
            a = jnp.concatenate([x_all[2 * i], x_all[2 * i + 1]], axis=1)
            b = jnp.concatenate([grad_all[gi, 2 * i], grad_all[gi, 2 * i + 1]], axis=0)
            sum_scr[...] += dot(a, b, 1, 0)
            return 0

        lax.fori_loop(0, n_sp // 2, one, 0)
        row_out[gi] = sum_scr[: n_dp * w_rows].astype(bf16)
        each_dp(lambda t: row_copy(gi, t, d).start())

    each_sp(lambda t: x_copy(s, t).wait_recv())
    weight_rows(0)
    reduce(1)

    def wait_pair(zb, _):
        pair_copy(zb, 1 - core).wait_recv()
        return 0

    lax.fori_loop(0, n_z, wait_pair, 0)
    mine = jnp.concatenate(
        [grad_all[0, s, :, :HEAD], grad_all[1, s, :, :HEAD], grad_all[0, s, :, HEAD:], grad_all[1, s, :, HEAD:]], axis=1
    )

    def inputs(j, _):
        r = span(j, block)
        ig_ref[:, r] = dot(mine, w_all[r], 1, 1).astype(bf16)
        return 0

    lax.fori_loop(0, n_dp, inputs, 0)
    weight_rows(1)

    for gi in range(2):

        def one(i, total):
            t = lax.rem(d + i, n_dp)
            row_copy(gi, d, t).wait_recv()
            return total + row_in[gi, t].astype(f32)

        total = lax.fori_loop(1, n_dp, one, row_out[gi, span(d, w_rows)].astype(f32)) * (1.0 / n_dp)
        wg_ref[:, gi * HEAD : (gi + 1) * HEAD] = total[:, :HEAD]
        wg_ref[:, (2 + gi) * HEAD : (3 + gi) * HEAD] = total[:, HEAD:]

    for gi in range(2):

        def sent_kv(t, _):
            kv_copy(gi, t, s).wait_send()
            return 0

        def sent_part(t, _):
            part_copy(gi, t, s).wait_send()
            return 0

        lax.fori_loop(s + 1, n_sp, sent_kv, 0)
        lax.fori_loop(0, s, sent_part, 0)
        each_sp(lambda t: grad_copy(gi, t, s).wait_send())
        each_dp(lambda t: row_copy(gi, t, d).wait_send())
    each_sp(lambda t: w_copy(t, s).wait_send())
    each_sp(lambda t: x_copy(t, s).wait_send())

    def sent_pair(zb, _):
        pair_copy(zb, core).wait_send()
        return 0

    lax.fori_loop(0, n_z, sent_pair, 0)
    for k in range(n_right):
        ring_copy(z, right, right_send.at[k]).wait_send()
    for k in range(n_left):
        ring_copy(z, left, left_send.at[k]).wait_send()


def body(layer_input, queries, keys, values, out_grad, key_value_weight):
    n_sp = lax.axis_size("sp")
    n_dp = lax.axis_size("dp")
    tokens, q_width = queries.shape
    width = layer_input.shape[1]
    w_rows, kv_width = key_value_weight.shape
    length = tokens * n_sp
    rows = HEADS_AT_ONCE * tokens
    sp_rows = width // n_sp
    sem = pltpu.SemaphoreType.DMA
    vmem = pl.BlockSpec(memory_space=pltpu.VMEM)
    return pl.pallas_call(
        functools.partial(kernel, n_dp, n_sp),
        out_shape=(
            jax.ShapeDtypeStruct((tokens, q_width), bf16),
            jax.ShapeDtypeStruct((tokens, width), bf16),
            jax.ShapeDtypeStruct((w_rows, kv_width), f32),
        ),
        in_specs=[vmem] * 6,
        out_specs=(vmem,) * 3,
        scratch_shapes=[
            pltpu.VMEM((length, rows), f32),
            pltpu.VMEM((length, rows), f32),
            pltpu.VMEM((length, HEAD), f32),
            pltpu.VMEM((length, HEAD), f32),
            pltpu.VMEM((HEAD, length), bf16),
            pltpu.VMEM((HEAD, rows), f32),
            pltpu.VMEM((2, length, 2 * HEAD), bf16),
            pltpu.VMEM((n_sp, sp_rows, tokens), bf16),
            pltpu.VMEM((n_sp, sp_rows, tokens), bf16),
            pltpu.VMEM((width, kv_width), bf16),
            pltpu.VMEM((2, n_sp, tokens, 2 * HEAD), bf16),
            pltpu.VMEM((2, n_sp, tokens, 2 * HEAD), bf16),
            pltpu.VMEM((2, n_sp, tokens, 2 * HEAD), bf16),
            pltpu.VMEM((max(sp_rows, tokens), 2 * HEAD), f32),
            pltpu.VMEM((2, sp_rows, 2 * HEAD), bf16),
            pltpu.VMEM((2, n_dp, w_rows, 2 * HEAD), bf16),
            sem((2, n_sp)), sem((2, n_sp)),
            sem((n_sp,)), sem((n_sp,)),
            sem((n_sp,)), sem((n_sp,)),
            sem((n_dp,)), sem((n_dp,)), sem((n_dp,)), sem((n_dp,)), sem((n_dp,)),
            sem((2, n_sp)), sem((2, n_sp)),
            sem((2, n_sp)), sem((2, n_sp)),
            sem((2, n_dp)), sem((2, n_dp)),
        ],
        compiler_params=pltpu.CompilerParams(
            collective_id=0, has_side_effects=True, vmem_limit_bytes=56 * 2**20
        ),
        cost_estimate=pl.CostEstimate(flops=12 * 2**30, bytes_accessed=8 * 2**20, transcendentals=8 * 2**20),
        name="attention_grads",
    )(layer_input, queries, keys, values, out_grad, key_value_weight)


def solution(mesh):
    placed = P(("dp", "sp"), None)
    return jax.shard_map(
        body,
        mesh=mesh,
        in_specs=(placed,) * 6,
        out_specs=(placed,) * 3,
        check_vma=False,
    )
```

time: 315 us -> 134 us (0.43)
  waiting for transfers between devices: 195 us -> 0 us
  Pallas kernels: 19.9 us -> 130 us
  blocking collectives: 62.1 us -> 0 us
  between operations: 13.8 us -> 0.65 us
  starting transfers between devices: 8.64 us -> 0 us
  matrix products: 7.8 us -> 0 us
  other arithmetic: 3.15 us -> 0 us
    all_gather x3 -> x0, waiting for transfers between devices: 195 us -> none  [the longest x1 108 us: body(): weight = lax.all_gather(key_value_weight, ('dp', 'sp'), axis=0, tiled=True)]
    pallas_call x1, Pallas kernels: 19.9 us -> 130 us  [body(): pl.pallas_call(functools.partial(kernel, n_dp, n_sp), out_shape=(jax.Shap...]
    all_to_all x2 -> x0, blocking collectives: 62.1 us -> none  [the longest x1 45.1 us: body(): lax.all_to_all(part.reshape(n_sp, tokens, 4 * HEAD), 'sp', split_axis=0,...]
    all_to_all x1 -> x0, starting transfers between devices: 8.52 us -> none  [body(): partial = lax.all_to_all(partial, 'dp', split_axis=0, concat_axis=0)]
    dot_general x2 -> x0, matrix products: 7.8 us -> none  [dot(): lax.dot_general(a, b, (((ca,), (cb,)), ((), ())), preferred_element_type=...]
  transfers between devices with their start and end apart: 4 -> 0, of which waited for: 3 -> 0; matrix products, arithmetic and copies ran while one was open for 3% -> 0% of each run, Pallas kernels for 0% -> 0%
where the time goes in v2:
time: 134 us
  Pallas kernels  130 us (97%)
  local copies, waits for them, and re-layouts  3.97 us (3%)
    pallas_call x1, Pallas kernels, body(): pl.pallas_call(functools.partial(kernel, n_dp, n_sp), out_shape=(jax.Shap...  130 us
    unnamed x7, local copies, waits for them, and re-layouts  3.97 us

profile of v2, /device:TPU:1, one launch (start us, length us, event | category | flops | bytes accessed | tf_op | source)
XLA Modules:
  0.0 134.3 jit_solution(8770986528694453254)
XLA Ops:
  0.6 129.7 %attention_grads.1 = (bf16[128,4096]{1,0:T(8,128)(2,1)}, bf16[128,4096]{1,0:T(8,128)(2,1)}, f32[16,512]{1,0:T(8,128)}) custom-call(bf16[128,4096]{1,0:T(8,128)(2,1)} %x_ref.1, bf16[128,4096]{1,0:T(8,128)(2,1)} %q_ref.1, bf16[128,256]{1,0:T(8,128)(2,1)} %k_ref.1, bf16[128,256]{1,0:T(8,128)(2,1)} %v_ref.1, bf16[128,4096]{1,0:T(8,128)(2,1)} %g_ref.1, ...), custom_call_target="tpu_custom_call" | custom-call | flops 12884901888 | bytes 8388608 | tf_op jit(solution)/shard_map/attention_grads/pallas_call | solution.py:403
  130.3 0.0 copy-start
  130.3 2.4 %copy.12 = bf16[128,4096]{1,0:T(8,128)(2,1)} copy(bf16[128,4096]{1,0:T(8,128)(2,1)} %get-tuple-element.6) | data formatting | bytes 2097152
  132.7 0.0 copy-done
  132.7 0.0 copy-start.1
  132.7 1.0 copy.13
  133.7 0.0 copy-done.1
  133.7 0.6 copy.14
Async XLA Ops:
  130.3 2.4 %copy-start = (bf16[128,4096]{1,0:T(8,128)(2,1)S(1)}, bf16[128,4096]{1,0:T(8,128)(2,1)}, u32[]{:S(2)}) copy-start(bf16[128,4096]{1,0:T(8,128)(2,1)} %get-tuple-element.7) | copy-start | bytes 3145732
  132.7 1.0 copy-start.1

commit v3 on v2

--- a/solution.py
+++ b/solution.py
@@ -92,17 +92,19 @@
 
 
 def kernel(
-    n_dp, n_sp,
+    n_dp, n_sp, n_y,
     x_ref, q_ref, k_ref, v_ref, g_ref, w_ref,
     dq_ref, ig_ref, wg_ref,
     s_scr, dp_scr, dk_scr, dv_scr, kt_scr, dqt_scr,
     kv_all, xt, x_all, w_all, part, part_in, grad_all, sum_scr, row_out, row_in,
     kv_send, kv_recv, x_send, x_recv, w_send, w_recv, right_send, left_send, ring_recv, pair_send, pair_recv,
-    part_send, part_recv, grad_send, grad_recv, row_send, row_recv,
+    part_send, part_recv, near_send, near_recv, far_send, far_recv, relay_send, relay_recv, row_send, row_recv,
 ):
     d = lax.axis_index("dp")
     s = lax.axis_index("sp")
     n_z = n_dp // 2
+    n_x = n_sp // n_y
+    sx, sy = s // n_y, s % n_y
     z, core = d // 2, d % 2
     tokens = q_ref.shape[0]
     length = tokens * n_sp
@@ -173,10 +175,76 @@
     def part_copy(gi, t, owner):
         return copy(part.at[gi, t], part_in.at[gi, owner], part_send.at[gi, t], part_recv.at[gi, owner], "sp", t)
 
-    def grad_copy(gi, t, owner):
-        return copy(
-            grad_all.at[gi, owner], grad_all.at[gi, owner], grad_send.at[gi, t], grad_recv.at[gi, owner], "sp", t
-        )
+    half_rows = tokens // 2
+    ring = (n_x, n_y)
+    at_ring = (sx, sy)
+
+    def place(h, far, near):
+        r = slice(h * half_rows, (h + 1) * half_rows)
+        return (far, near, r) if h == 0 else (near, far, r)
+
+    def partner(h, i, last):
+        return i * n_y + sy if (h == 0) == last else sx * n_y + i
+
+    def near_copy(gi, h, i, owner):
+        ref = grad_all.at[(gi,) + place(h, at_ring[h], owner)]
+        return copy(ref, ref, near_send.at[gi, h, i], near_recv.at[gi, h, owner], "sp", partner(h, i, False))
+
+    def far_copy(gi, h, side, owner):
+        ref = grad_all.at[(gi,) + place(h, owner, slice(None))]
+        to = lax.rem(at_ring[h] + (1, ring[h] - 1)[side], ring[h])
+        return copy(ref, ref, far_send.at[gi, h, side], far_recv.at[gi, h, side], "sp", partner(h, to, True))
+
+    def relay_copy(gi, h, side, owner):
+        middle = ring[1 - h] // 2
+        which = slice(0, middle) if side == 0 else slice(middle, ring[1 - h])
+        ref = grad_all.at[(gi,) + place(h, owner, which)]
+        to = lax.rem(at_ring[h] + (1, ring[h] - 1)[side], ring[h])
+        return copy(ref, ref, relay_send.at[gi, h, side], relay_recv.at[gi, h, side], "sp", partner(h, to, True))
+
+    def others(h, f):
+        def one(i, _):
+            f(lax.rem(at_ring[1 - h] + i, ring[1 - h]))
+            return 0
+
+        lax.fori_loop(1, ring[1 - h], one, 0)
+
+    def sides(h):
+        return min(ring[h] - 1, 2)
+
+    def behind(h, side, n):
+        return lax.rem(at_ring[h] + ring[h] + (-n, n)[side], ring[h])
+
+    def gather_near(gi):
+        for h in range(2):
+            others(h, lambda i: near_copy(gi, h, i, at_ring[1 - h]).start())
+
+    def gather_far(gi):
+        for h in range(2):
+            others(h, lambda i: near_copy(gi, h, at_ring[1 - h], i).wait_recv())
+            for side in range(sides(h)):
+                far_copy(gi, h, side, at_ring[h]).start()
+
+    def gather_relay(gi):
+        for h in range(2):
+            for side in range(sides(h)):
+                far_copy(gi, h, side, behind(h, side, 1)).wait_recv()
+                if ring[h] == 4:
+                    relay_copy(gi, h, side, behind(h, side, 1)).start()
+
+    def gather_end(gi):
+        for h in range(2):
+            if ring[h] == 4:
+                for side in range(2):
+                    relay_copy(gi, h, side, behind(h, side, 2)).wait_recv()
+
+    def gather_sent(gi):
+        for h in range(2):
+            others(h, lambda i: near_copy(gi, h, i, at_ring[1 - h]).wait_send())
+            for side in range(sides(h)):
+                far_copy(gi, h, side, at_ring[h]).wait_send()
+                if ring[h] == 4:
+                    relay_copy(gi, h, side, behind(h, side, 1)).wait_send()
 
     def row_copy(gi, t, owner):
         return copy(
@@ -193,17 +261,6 @@
 
         lax.fori_loop(s + 1, n_sp, clear, 0)
     w_all[pl.ds(pl.multiple_of(d * block + s * w_rows, w_rows), w_rows)] = w_ref[...]
-    pl.semaphore_wait(barrier, n_sp + n_dp - 2)
-
-    for gi in range(2):
-
-        def send_kv(t, _):
-            kv_copy(gi, t, s).start()
-            return 0
-
-        lax.fori_loop(s + 1, n_sp, send_kv, 0)
-    each_sp(lambda t: w_copy(t, s).start())
-
     def transpose(j, _):
         columns = x_ref[:, span(j, block)].T
         xt[:, span(j, w_rows)] = columns.reshape(n_sp, w_rows, tokens)
@@ -211,7 +268,24 @@
 
     lax.fori_loop(0, n_dp, transpose, 0)
     x_all[s] = xt[s]
-    each_sp(lambda t: x_copy(t, s).start())
+    pl.semaphore_wait(barrier, n_sp + n_dp - 2)
+
+    def send_kv(gi):
+        def one(t, _):
+            kv_copy(gi, t, s).start()
+            return 0
+
+        lax.fori_loop(s + 1, n_sp, one, 0)
+
+    def sent_kv(gi):
+        def one(t, _):
+            kv_copy(gi, t, s).wait_send()
+            return 0
+
+        lax.fori_loop(s + 1, n_sp, one, 0)
+
+    send_kv(0)
+
 
     right = lax.rem(z + 1, n_z)
     left = lax.rem(z + n_z - 1, n_z)
@@ -222,7 +296,8 @@
         @pl.when(k == 0)
         def _():
             each_sp(lambda t: w_copy(s, t).wait_recv())
-            ring_copy(z, right, right_send.at[0]).start()
+            if n_right:
+                ring_copy(z, right, right_send.at[0]).start()
             if n_left:
                 ring_copy(z, left, left_send.at[0]).start()
             pair_copy(z, core).start()
@@ -257,8 +332,8 @@
 
         sum_scr[:tokens] = part[gi, s].astype(f32)
         lax.fori_loop(s + 1, n_sp, one, 0)
-        grad_all[gi, s] = sum_scr[:tokens].astype(bf16)
-        each_sp(lambda t: grad_copy(gi, t, s).start())
+        grad_all[gi, sx, sy] = sum_scr[:tokens].astype(bf16)
+        gather_near(gi)
 
     steps = 2 * per_group
     for gi in range(2):
@@ -281,15 +356,31 @@
         def heads(hb, _):
             it = gi * per_group + hb
 
-            @pl.when(it >= 1)
+            if gi == 0:
+
+                @pl.when(hb == 0)
+                def _():
+                    sent_kv(0)
+                    send_kv(1)
+                    each_sp(lambda t: w_copy(t, s).start())
+
+            @pl.when(it == 1)
             def _():
-                ring_step(it - 1)
+                each_sp(lambda t: x_copy(t, s).start())
+
+            @pl.when(it % 2 == 1)
+            def _():
+                ring_step(it // 2)
 
             if gi == 1:
 
-                @pl.when(it == steps * 3 // 4)
+                @pl.when(it == steps - 2)
                 def _():
                     reduce(0)
+
+                @pl.when(it == steps - 1)
+                def _():
+                    gather_far(0)
 
             attend_heads(
                 s, gi * group + hb * HEADS_AT_ONCE, key_rows,
@@ -312,16 +403,18 @@
 
         lax.fori_loop(0, s + 1, give, 0)
 
-    for k in range(steps - 1, n_right + 1):
+    for k in range(steps // 2, n_right + 1):
         ring_step(k)
+    gather_relay(0)
 
     def weight_rows(gi):
-        each_sp(lambda t: grad_copy(gi, s, t).wait_recv())
+        gather_end(gi)
         sum_scr[...] = jnp.zeros_like(sum_scr)
 
         def one(i, _):
             a = jnp.concatenate([x_all[2 * i], x_all[2 * i + 1]], axis=1)
-            b = jnp.concatenate([grad_all[gi, 2 * i], grad_all[gi, 2 * i + 1]], axis=0)
+            j = 2 * i
+            b = jnp.concatenate([grad_all[gi, j // n_y, j % n_y], grad_all[gi, j // n_y, j % n_y + 1]], axis=0)
             sum_scr[...] += dot(a, b, 1, 0)
             return 0
 
@@ -339,7 +432,7 @@
 
     lax.fori_loop(0, n_z, wait_pair, 0)
     mine = jnp.concatenate(
-        [grad_all[0, s, :, :HEAD], grad_all[1, s, :, :HEAD], grad_all[0, s, :, HEAD:], grad_all[1, s, :, HEAD:]], axis=1
+        [grad_all[gi, sx, sy, :, c] for c in (slice(0, HEAD), slice(HEAD, 2 * HEAD)) for gi in range(2)], axis=1
     )
 
     def inputs(j, _):
@@ -347,7 +440,10 @@
         ig_ref[:, r] = dot(mine, w_all[r], 1, 1).astype(bf16)
         return 0
 
-    lax.fori_loop(0, n_dp, inputs, 0)
+    lax.fori_loop(0, n_dp // 2, inputs, 0)
+    gather_far(1)
+    lax.fori_loop(n_dp // 2, n_dp, inputs, 0)
+    gather_relay(1)
     weight_rows(1)
 
     for gi in range(2):
@@ -363,18 +459,14 @@
 
     for gi in range(2):
 
-        def sent_kv(t, _):
-            kv_copy(gi, t, s).wait_send()
-            return 0
-
         def sent_part(t, _):
             part_copy(gi, t, s).wait_send()
             return 0
 
-        lax.fori_loop(s + 1, n_sp, sent_kv, 0)
         lax.fori_loop(0, s, sent_part, 0)
-        each_sp(lambda t: grad_copy(gi, t, s).wait_send())
+        gather_sent(gi)
         each_dp(lambda t: row_copy(gi, t, d).wait_send())
+    sent_kv(1)
     each_sp(lambda t: w_copy(t, s).wait_send())
     each_sp(lambda t: x_copy(t, s).wait_send())
 
@@ -392,6 +484,7 @@
 def body(layer_input, queries, keys, values, out_grad, key_value_weight):
     n_sp = lax.axis_size("sp")
     n_dp = lax.axis_size("dp")
+    n_y = 4 if n_sp % 4 == 0 and n_sp > 8 else 2
     tokens, q_width = queries.shape
     width = layer_input.shape[1]
     w_rows, kv_width = key_value_weight.shape
@@ -401,7 +494,7 @@
     sem = pltpu.SemaphoreType.DMA
     vmem = pl.BlockSpec(memory_space=pltpu.VMEM)
     return pl.pallas_call(
-        functools.partial(kernel, n_dp, n_sp),
+        functools.partial(kernel, n_dp, n_sp, n_y),
         out_shape=(
             jax.ShapeDtypeStruct((tokens, q_width), bf16),
             jax.ShapeDtypeStruct((tokens, width), bf16),
@@ -422,7 +515,7 @@
             pltpu.VMEM((width, kv_width), bf16),
             pltpu.VMEM((2, n_sp, tokens, 2 * HEAD), bf16),
             pltpu.VMEM((2, n_sp, tokens, 2 * HEAD), bf16),
-            pltpu.VMEM((2, n_sp, tokens, 2 * HEAD), bf16),
+            pltpu.VMEM((2, n_sp // n_y, n_y, tokens, 2 * HEAD), bf16),
             pltpu.VMEM((max(sp_rows, tokens), 2 * HEAD), f32),
             pltpu.VMEM((2, sp_rows, 2 * HEAD), bf16),
             pltpu.VMEM((2, n_dp, w_rows, 2 * HEAD), bf16),
@@ -431,7 +524,9 @@
             sem((n_sp,)), sem((n_sp,)),
             sem((n_dp,)), sem((n_dp,)), sem((n_dp,)), sem((n_dp,)), sem((n_dp,)),
             sem((2, n_sp)), sem((2, n_sp)),
-            sem((2, n_sp)), sem((2, n_sp)),
+            sem((2, 2, n_sp)), sem((2, 2, n_sp)),
+            sem((2, 2, 2)), sem((2, 2, 2)),
+            sem((2, 2, 2)), sem((2, 2, 2)),
             sem((2, n_dp)), sem((2, n_dp)),
         ],
         compiler_params=pltpu.CompilerParams(

time: 134 us -> 133 us (level)
  Pallas kernels: 130 us -> 128 us
    pallas_call x1, Pallas kernels: 130 us -> 128 us  [body(): pl.pallas_call(functools.partial(kernel, n_dp, n_sp, n_y), out_shape=(jax...]
where the time goes in v3:
time: 133 us
  Pallas kernels  128 us (96%)
  local copies, waits for them, and re-layouts  3.97 us (3%)
    pallas_call x1, Pallas kernels, body(): pl.pallas_call(functools.partial(kernel, n_dp, n_sp, n_y), out_shape=(jax...  128 us
    unnamed x7, local copies, waits for them, and re-layouts  3.97 us

profile of v3, /device:TPU:1, one launch (start us, length us, event | category | flops | bytes accessed | tf_op | source)
XLA Modules:
  0.0 132.9 jit_solution(16512689142706364139)
XLA Ops:
  0.6 128.3 %attention_grads.1 = (bf16[128,4096]{1,0:T(8,128)(2,1)}, bf16[128,4096]{1,0:T(8,128)(2,1)}, f32[16,512]{1,0:T(8,128)}) custom-call(bf16[128,4096]{1,0:T(8,128)(2,1)} %x_ref.1, bf16[128,4096]{1,0:T(8,128)(2,1)} %q_ref.1, bf16[128,256]{1,0:T(8,128)(2,1)} %k_ref.1, bf16[128,256]{1,0:T(8,128)(2,1)} %v_ref.1, bf16[128,4096]{1,0:T(8,128)(2,1)} %g_ref.1, ...), custom_call_target="tpu_custom_call" | custom-call | flops 12884901888 | bytes 8388608 | tf_op jit(solution)/shard_map/attention_grads/pallas_call | solution.py:496
  128.9 0.0 copy-start
  128.9 2.4 %copy.12 = bf16[128,4096]{1,0:T(8,128)(2,1)} copy(bf16[128,4096]{1,0:T(8,128)(2,1)} %get-tuple-element.6) | data formatting | bytes 2097152
  131.3 0.0 copy-done
  131.3 0.0 copy-start.1
  131.3 1.0 copy.13
  132.3 0.0 copy-done.1
  132.3 0.6 copy.14
Async XLA Ops:
  128.9 2.4 %copy-start = (bf16[128,4096]{1,0:T(8,128)(2,1)S(1)}, bf16[128,4096]{1,0:T(8,128)(2,1)}, u32[]{:S(2)}) copy-start(bf16[128,4096]{1,0:T(8,128)(2,1)} %get-tuple-element.7) | copy-start | bytes 3145732
  131.3 1.0 copy-start.1
